TPU v7x, 256 devices: a whole 4x4x8 slice. The times are simulated.
256 devices in a mesh: dp: 32 (over x, y, core), mp: 8 (over z).
Axes of the slice: x: 4, y: 4, z: 8, core: 2. Of those that a mesh axis runs over, the one named last changes fastest.
Arguments:
- queries: bfloat16 [4096, 4096], P('dp', 'mp'), may hold values from -100 to 100
- neighbours: bfloat16 [128, 256, 896], P(None, 'dp'), may hold values from -6 to 6
- targets: int32 [256], P('dp'), may hold values from 0 to 127, as said below
- counts: int32 [32], P('dp'), may hold values from 0 to 8, as said below
- in_weight: bfloat16 [896, 3584], P(None, 'mp'), may hold values from -0.1875 to 0.1875
- out_weight: bfloat16 [3584, 896], P('mp'), may hold values from -0.09375 to 0.09375
- kv_weight: bfloat16 [896, 2, 4096], P(None, None, 'mp'), may hold values from -0.1875 to 0.1875
- d_context: bfloat16 [4096, 4096], P('dp', 'mp'), may hold values from -6 to 6
Outputs:
- context: bfloat16 [4096, 4096], P('dp', 'mp')
- d_queries: bfloat16 [4096, 4096], P('dp', 'mp')
- grad_kv: float32 [896, 2, 4096], P('dp', None, 'mp')
- grad_in: float32 [896, 3584], P('dp', 'mp')
- grad_out: float32 [3584, 896], P('mp', 'dp')
Inputs may be any that keep to these rules, and one draw needn't show every extreme that they name: Every block index o * 4 + p (o an owner, p < 4) is the target of exactly one live slot over all holders; at most 1 live slots of one holder target one owner, and some holder reaches 1; targets of slots that are not live are arbitrary. counts sum to 4 times the number of devices along dp.
All inputs are finite; a program needn't handle non-finite values.
Results may differ from a plain program's by a relative error of at most 0.04.
Values may be sent and summed in bfloat16 or wider, within the bound.
No kernel may reach another device: no remote copies, remote signals or barrier semaphores. Data moves between devices by JAX's collectives and lax.ppermute only.
A program may use at most 64 MiB of HBM per device.

v0:
```python
import jax
import jax.numpy as jnp
from jax import lax
from jax.sharding import PartitionSpec as P

DH = 128
SPAN = 64
NEIGH = 2


GELU_C = 0.7978845608028654
GELU_A = 0.044715
EPSILON = 1e-06


def gelu_value(values):
    inner = GELU_C * (values + GELU_A * values * values * values)
    return 0.5 * values * (1.0 + jnp.tanh(inner))


def gelu_slope(values):
    inner = GELU_C * (values + GELU_A * values * values * values)
    tanh_value = jnp.tanh(inner)
    return 0.5 * (1.0 + tanh_value) + 0.5 * values * (1.0 - tanh_value * tanh_value) * GELU_C * (
        1.0 + 3.0 * GELU_A * values * values
    )


def rms_normed(rows):
    wide = rows.astype(jnp.float32)
    mean_square = jnp.mean(wide * wide, axis=-1, keepdims=True)
    return (wide * lax.rsqrt(mean_square + EPSILON)).astype(jnp.bfloat16)


def encode_front(rows, in_weight):
    length, spread, columns = rows.shape
    normed = rms_normed(rows).reshape(length * spread, columns)
    hidden_pre = jnp.dot(normed, in_weight, preferred_element_type=jnp.float32)
    activated = gelu_value(hidden_pre).astype(jnp.bfloat16)
    return (normed, hidden_pre, activated)


def to_spans(values, spans):
    length, blocks, columns = values.shape
    heads = columns // DH
    return (
        values.reshape(length, spans, 2, heads, DH)
        .transpose(1, 2, 0, 3, 4)
        .reshape(spans, 2 * length, heads, DH)
    )


def from_spans(values, length):
    spans, keys_len, heads, depth = values.shape
    return (
        values.reshape(spans, 2, length, heads, depth)
        .transpose(2, 0, 1, 3, 4)
        .reshape(length, 2 * spans, heads * depth)
    )


def attend(queries, keys, values, grads):
    scaling = DH ** (-0.5)
    scores = (
        jnp.einsum("cqhd,ckhd->chqk", queries, keys, preferred_element_type=jnp.float32) * scaling
    )
    peak = jnp.max(scores, axis=-1, keepdims=True)
    weights = jnp.exp(scores - peak)
    probs_wide = weights / jnp.sum(weights, axis=-1, keepdims=True)
    probs = probs_wide.astype(jnp.bfloat16)
    context = jnp.einsum(
        "chqk,ckhd->cqhd", probs, values, preferred_element_type=jnp.float32
    ).astype(jnp.bfloat16)
    d_probs = jnp.einsum("cqhd,ckhd->chqk", grads, values, preferred_element_type=jnp.float32)
    d_scores = (
        probs_wide * (d_probs - jnp.sum(d_probs * probs_wide, axis=-1, keepdims=True)) * scaling
    ).astype(jnp.bfloat16)
    d_queries = jnp.einsum(
        "chqk,ckhd->cqhd", d_scores, keys, preferred_element_type=jnp.float32
    ).astype(jnp.bfloat16)
    d_keys = jnp.einsum(
        "chqk,cqhd->ckhd", d_scores, queries, preferred_element_type=jnp.float32
    ).astype(jnp.bfloat16)
    d_values = jnp.einsum(
        "chqk,cqhd->ckhd", probs, grads, preferred_element_type=jnp.float32
    ).astype(jnp.bfloat16)
    return (context, d_queries, d_keys, d_values)


def per_device(queries, neighbours, targets, counts, in_weight, out_weight, kv_weight, d_context):
    length, holding, enc_width = neighbours.shape
    devices_dp = lax.axis_size("dp")
    devices_mp = lax.axis_size("mp")
    slice_rows = length // devices_mp
    token_rows, local_columns = queries.shape
    spans = token_rows // SPAN
    blocks = NEIGH * spans
    capacity = max(1, 2 * blocks // devices_dp)
    my_rank = lax.axis_index("mp")
    slot_ids = jnp.arange(holding, dtype=jnp.int32)
    is_live = slot_ids < counts[0]
    dest_owner = targets // blocks
    slot_place = targets % blocks
    owner_hits = jnp.logical_and(
        dest_owner[:, None] == jnp.arange(devices_dp, dtype=jnp.int32)[None, :], is_live[:, None]
    ).astype(jnp.int32)
    earlier = jnp.cumsum(owner_hits, axis=0) - owner_hits
    ranking = jnp.sum(earlier * owner_hits, axis=1)
    dest_slot = jnp.where(is_live, dest_owner * capacity + ranking, -1)
    selector_ints = (
        jnp.arange(devices_dp * capacity, dtype=jnp.int32)[:, None] == dest_slot[None, :]
    ).astype(jnp.int32)
    selector = selector_ints.astype(jnp.bfloat16)
    filled = jnp.sum(selector_ints, axis=1) > 0
    sent_place = jnp.where(filled, jnp.sum(selector_ints * slot_place[None, :], axis=1), -1)
    sent_place = sent_place.reshape(1, devices_dp, capacity, 1)
    own_slice = lax.dynamic_slice_in_dim(neighbours, my_rank * slice_rows, slice_rows, 0)
    normed, hidden_pre, activated = encode_front(neighbours, in_weight)
    picked = activated
    summed = lax.psum_scatter(
        jnp.dot(picked, out_weight, preferred_element_type=jnp.float32)
        .reshape(slice_rows * lax.axis_size("mp"), holding, enc_width)
        .astype(jnp.bfloat16),
        "mp",
        scatter_dimension=0,
        tiled=True,
    ).astype(jnp.float32)
    encoded = (own_slice.astype(jnp.float32) + summed).astype(jnp.bfloat16)
    moved = jnp.einsum("kh,thd->tkd", selector, encoded, preferred_element_type=jnp.float32).astype(
        jnp.bfloat16
    )
    received = lax.all_to_all(
        moved.reshape(slice_rows, devices_dp, capacity, enc_width),
        "dp",
        split_axis=1,
        concat_axis=1,
        tiled=True,
    )
    received_place = lax.all_to_all(sent_place, "dp", split_axis=1, concat_axis=1, tiled=True)
    placing = (
        received_place.reshape(1, -1) == jnp.arange(blocks, dtype=jnp.int32)[:, None]
    ).astype(jnp.bfloat16)
    rows = jnp.einsum(
        "bk,tkd->tbd",
        placing,
        received.reshape(slice_rows, -1, enc_width),
        preferred_element_type=jnp.float32,
    )
    slices, placing = (rows.astype(jnp.bfloat16), placing)
    piece = lax.all_gather(slices, "mp", axis=0, tiled=True)
    projected = jnp.einsum(
        "tbe,ejx->tbjx", piece, kv_weight, preferred_element_type=jnp.float32
    ).astype(jnp.bfloat16)
    gathered = piece
    heads = local_columns // DH
    heads_queries = queries.reshape(spans, SPAN, heads, DH)
    heads_grads = d_context.reshape(spans, SPAN, heads, DH)
    context, d_queries, d_keys, d_values = attend(
        heads_queries,
        to_spans(projected[:, :, 0], spans),
        to_spans(projected[:, :, 1], spans),
        heads_grads,
    )
    d_keyvals = jnp.stack([from_spans(d_keys, length), from_spans(d_values, length)], axis=2)
    picked = d_keyvals
    d_slices = lax.psum_scatter(
        jnp.einsum("tbjx,ejx->tbe", picked, kv_weight, preferred_element_type=jnp.float32).astype(
            jnp.bfloat16
        ),
        "mp",
        scatter_dimension=0,
        tiled=True,
    )
    kv_terms = jnp.einsum("tbe,tbjx->ejx", gathered, d_keyvals, preferred_element_type=jnp.float32)
    grad_kv = lax.psum_scatter(
        kv_terms.astype(jnp.bfloat16), "dp", scatter_dimension=0, tiled=True
    ).astype(jnp.float32)
    returned = jnp.einsum(
        "bk,tbd->tkd", placing, d_slices, preferred_element_type=jnp.float32
    ).astype(jnp.bfloat16)
    returned = returned.reshape(slice_rows, devices_dp, capacity, enc_width)
    back_home = lax.all_to_all(returned, "dp", split_axis=1, concat_axis=1, tiled=True)
    slot_grads = jnp.einsum(
        "kh,tkd->thd",
        selector,
        back_home.reshape(slice_rows, -1, enc_width),
        preferred_element_type=jnp.float32,
    ).astype(jnp.bfloat16)
    piece = lax.all_gather(slot_grads, "mp", axis=0, tiled=True)
    count = piece.shape[0]
    spread = piece.shape[1]
    flat = piece.reshape(count * spread, enc_width)
    d_act = jnp.einsum("ne,fe->nf", flat, out_weight, preferred_element_type=jnp.float32)
    d_pre = (d_act * gelu_slope(hidden_pre)).astype(jnp.bfloat16)
    in_total = jnp.einsum("ne,nf->ef", normed, d_pre, preferred_element_type=jnp.float32)
    out_total = jnp.einsum("ne,nf->ef", flat, activated, preferred_element_type=jnp.float32)
    in_total, out_total = (in_total, out_total)
    grad_in, grad_out_t = (
        lax.psum_scatter(
            in_total.astype(jnp.bfloat16), "dp", scatter_dimension=0, tiled=True
        ).astype(jnp.float32),
        lax.psum_scatter(
            out_total.astype(jnp.bfloat16), "dp", scatter_dimension=0, tiled=True
        ).astype(jnp.float32),
    )
    return (
        context.reshape(token_rows, local_columns),
        d_queries.reshape(token_rows, local_columns),
        grad_kv,
        grad_in,
        grad_out_t.T,
    )


def solution(mesh):
    placed = (
        P("dp", "mp"),
        P(None, "dp", None),
        P("dp"),
        P("dp"),
        P(None, "mp"),
        P("mp", None),
        P(None, None, "mp"),
        P("dp", "mp"),
    )
    return jax.shard_map(
        per_device,
        mesh=mesh,
        in_specs=placed,
        out_specs=(P("dp", "mp"), P("dp", "mp"), P("dp", None, "mp"), P("dp", "mp"), P("mp", "dp")),
        check_vma=False,
    )
```

profile of v0, /device:TPU:12, one launch (start us, length us, event | category | flops | bytes accessed | tf_op | source)
XLA Modules:
  0.0 428.9 jit_solution(4433793728126517260)
XLA Ops:
  17.6 7.5 %all-to-all-start.1 = ((s32[1,32,1,1]{3,2,0,1:T(1,128)}), s32[1,32,1,1]{3,2,0,1:T(1,128)S(1)}, u32[]{:S(2)}, u32[]{:S(2)}) async-start(s32[1,32,1,1]{3,2,0,1:T(1,128)} %copy.128), calls=%async_computation.2 | async-start | bytes 32768 | tf_op jit(solution)/shard_map/all_to_all | solution.py:139
  25.1 35.0 %reduce-scatter.6.cloned.1.call-done = bf16[16,8,896]{2,1,0:T(8,128)(2,1)} async-done(((bf16[128,8,896]{2,1,0:T(8,128)(2,1)}), bf16[16,8,896]{2,1,0:T(8,128)(2,1)}) %reduce-scatter.6.cloned.1.call-update) | async-done | bytes 229392 | tf_op jit(solution)/shard_map/reduce_scatter | solution.py:120
  63.4 7.6 %all-to-all-start = ((bf16[16,32,1,896]{3,0,2,1:T(8,128)(2,1)}), bf16[16,32,1,896]{3,0,2,1:T(8,128)(2,1)S(1)}, u32[]{:S(2)}, u32[]{:S(2)}) async-start(bf16[16,32,1,896]{3,0,2,1:T(8,128)(2,1)} %copy.126), calls=%async_computation.1 | async-start | bytes 1835008 | tf_op jit(solution)/shard_map/all_to_all | solution.py:132
  76.1 7.2 %all-to-all-done = bf16[16,32,1,896]{3,0,2,1:T(8,128)(2,1)S(1)} async-done(((bf16[16,32,1,896]{3,0,2,1:T(8,128)(2,1)}), bf16[16,32,1,896]{3,0,2,1:T(8,128)(2,1)S(1)}, u32[]{:S(2)}, u32[]{:S(2)}) %all-to-all-start) | async-done | bytes 917536 | tf_op jit(solution)/shard_map/all_to_all | solution.py:132
  84.4 26.8 %all_gather.6 = bf16[128,4,896]{2,1,0:T(4,128)(2,1)S(1)} all-gather(bf16[16,4,896]{2,1,0:T(4,128)(2,1)S(1)} %fusion.52), channel_id=1, replica_groups=mesh['dp'=32,'mp'=8] {'mp'}, dimensions={0}, use_global_device_ids=true | all-gather | bytes 1032192 | tf_op jit(solution)/shard_map/all_gather | solution.py:150
  122.9 3.3 convolution_convert_fusion.2
  126.2 5.6 %convolution_convert_fusion.3 = bf16[2,4,256,128]{3,2,1,0:T(8,128)(2,1)} fusion(f32[2,4,64,256]{3,2,1,0:T(8,128)} %convolution_bitcast_fusion, bf16[2,64,4,128]{3,2,1,0:T(4,128)(2,1)S(1)} %copy-done.4, f32[2,4,64,256]{3,2,1,0:T(8,128)} %get-tuple-element.28, f32[2,4,64]{2,1,0:T(4,128)S(1)} %get-tuple-element.27), kind=kOutput, calls=%fused_computation.39 | convolution fusion | flops 34734848 | bytes 1705984 | tf_op jit(solution)/shard_map/chqk,cqhd->ckhd/dot_general | solution.py:81
  144.2 3.1 bitcast_convert_fusion.1
  150.4 72.1 %all-reduce.12.cloned.1.call-done = bf16[128,4,896]{2,1,0:T(4,128)(2,1)} async-done(((bf16[128,4,896]{2,1,0:T(4,128)(2,1)}), bf16[128,4,896]{2,1,0:T(4,128)(2,1)}) %all-reduce.12.cloned.1.call-update) | async-done | bytes 917520
  224.1 19.6 %all_to_all.15 = bf16[16,32,1,896]{3,0,2,1:T(8,128)(2,1)S(1)} all-to-all(bf16[16,32,1,896]{3,0,2,1:T(8,128)(2,1)S(1)} %copy.145), channel_id=1, replica_groups=mesh['dp'=32,'mp'=8] {'dp'}, dimensions={1} | all-to-all | bytes 1835008 | tf_op jit(solution)/shard_map/all_to_all | solution.py:182
  246.8 4.3 %fusion.51 = bf16[2,64,4,128]{3,1,2,0:T(8,128)(2,1)S(1)} fusion(bf16[2,256,4,128]{3,1,2,0:T(8,128)(2,1)} %bitcast.131, f32[2,4,64,256]{3,2,1,0:T(8,128)} %convolution_bitcast_fusion, f32[2,4,64,256]{3,2,1,0:T(8,128)} %get-tuple-element.28, f32[2,4,64]{2,1,0:T(4,128)S(1)} %get-tuple-element.27), kind=kOutput, calls=%fused_computation.55 | convolution fusion | flops 34538240 | bytes 1705984 | tf_op jit(solution)/shard_map/chqk,ckhd->cqhd/dot_general | solution.py:78
  256.3 3.2 copy.142
  260.2 22.8 %all-gather.2.cloned.1.call-done = bf16[128,8,896]{2,1,0:T(8,128)(2,1)} async-done(((bf16[16,8,896]{2,1,0:T(8,128)(2,1)}), bf16[128,8,896]{2,1,0:T(8,128)(2,1)}) %all-gather.2.cloned.1.call-update) | async-done | bytes 1835024 | tf_op jit(solution)/shard_map/all_gather | solution.py:189
  283.0 4.3 %fusion.30 = bf16[896,448]{1,0:T(8,128)(2,1)S(1)} fusion(bf16[128,8,896]{2,1,0:T(8,128)(2,1)S(1)} %copy-done.1, f32[128,8]{1,0:T(8,128)} %copy-done.6, f32[1024,448]{0,1:T(8,128)} %copy-done.15, bf16[448,896]{1,0:T(8,128)(2,1)S(1)} %copy-done, bf16[128,8,896]{2,1,0:T(8,128)(2,1)} %all-gather.2.cloned.1.call-done), kind=kOutput, calls=%fused_computation.32 | convolution fusion | flops 1656037376 | bytes 7114752 | tf_op jit(solution)/shard_map/ne,nf->ef/dot_general | solution.py:195
  287.3 3.3 fusion.35
  290.6 62.2 %fusion.100 = (bf16[32,448]{1,0:T(8,128)(2,1)S(1)}, bf16[32,448]{1,0:T(8,128)(2,1)S(1)}) fusion(bf16[896,448]{1,0:T(8,128)(2,1)S(1)} %fusion.30, bf16[896,448]{1,0:T(8,128)(2,1)S(1)} %fusion.35), kind=kCustom, calls=%all-reduce-scatter.2 | all-reduce-scatter fusion | flops 917505 | bytes 1664000
  354.8 5.1 %collective-permute-start.1 = (bf16[32,448]{1,0:T(8,128)(2,1)S(1)}, bf16[32,448]{1,0:T(8,128)(2,1)S(1)}, u32[]{:S(2)}, u32[]{:S(2)}) collective-permute-start(bf16[32,448]{1,0:T(8,128)(2,1)S(1)} %get-tuple-element.19), channel_id=1, source_target_pairs={{0,16},{8,24},{16,32},{24,40},{32,48},{40,56},{48,64},{56,72},{64,... | collective-permute-start | bytes 86024
  359.9 5.3 %collective-permute-start = (bf16[32,448]{1,0:T(8,128)(2,1)S(1)}, bf16[32,448]{1,0:T(8,128)(2,1)S(1)}, u32[]{:S(2)}, u32[]{:S(2)}) collective-permute-start(bf16[32,448]{1,0:T(8,128)(2,1)S(1)} %get-tuple-element.19), channel_id=1, source_target_pairs={{0,8},{8,16},{16,24},{24,32},{32,40},{40,48},{48,56},{56,64},{64,7... | collective-permute-start | bytes 86024
  365.3 3.5 collective-permute-start.3
  368.8 32.3 %all-reduce.10.cloned.1.call-done = bf16[896,2,512]{2,1,0:T(2,128)(2,1)} async-done(((bf16[896,2,512]{2,1,0:T(2,128)(2,1)}), bf16[896,2,512]{2,1,0:T(2,128)(2,1)}) %all-reduce.10.cloned.1.call-update) | async-done | bytes 1835024
  404.6 4.5 %collective-permute-start.5 = (bf16[32,448]{1,0:T(8,128)(2,1)S(1)}, bf16[32,448]{1,0:T(8,128)(2,1)S(1)}, u32[]{:S(2)}, u32[]{:S(2)}) collective-permute-start(bf16[32,448]{1,0:T(8,128)(2,1)S(1)} %get-tuple-element.20), channel_id=1, source_target_pairs={{0,16},{8,24},{16,32},{24,40},{32,48},{40,56},{48,64},{56,72},{64,... | collective-permute-start | bytes 86024
  409.1 3.8 collective-permute-start.4
  412.9 2.7 collective-permute-start.7
  416.9 4.2 collective-permute-done.7
  (104 shorter events, 62.7 us)
Async XLA Ops:
  7.2 6.0 %copy-start = (bf16[448,896]{1,0:T(8,128)(2,1)S(1)}, bf16[448,896]{1,0:T(8,128)(2,1)}, u32[]{:S(2)}) copy-start(bf16[448,896]{1,0:T(8,128)(2,1)} %param.13) | copy-start | bytes 2408452
  7.2 2.3 copy-start.1
  7.2 52.9 %reduce-scatter.6.cloned.1.call-start = ((), (), s32[]{:S(2)}) async-start(), calls=%async_computation.4 | async-start | bytes 2064384 | tf_op jit(solution)/shard_map/reduce_scatter | solution.py:120
  9.5 2.4 copy-start.6
  16.8 45.9 %copy-start.8 = (s32[8]{0:T(128)}, s32[8]{0:T(128)S(1)}, u32[]{:S(2)}) copy-start(s32[8]{0:T(128)S(1)} %add_select_fusion) | copy-start | bytes 100
  17.6 45.1 %all-to-all-start.1 = ((s32[1,32,1,1]{3,2,0,1:T(1,128)}), s32[1,32,1,1]{3,2,0,1:T(1,128)S(1)}, u32[]{:S(2)}, u32[]{:S(2)}) async-start(s32[1,32,1,1]{3,2,0,1:T(1,128)} %copy.128), calls=%async_computation.2 | async-start | bytes 32768 | tf_op jit(solution)/shard_map/all_to_all | solution.py:139
  63.4 20.0 %all-to-all-start = ((bf16[16,32,1,896]{3,0,2,1:T(8,128)(2,1)}), bf16[16,32,1,896]{3,0,2,1:T(8,128)(2,1)S(1)}, u32[]{:S(2)}, u32[]{:S(2)}) async-start(bf16[16,32,1,896]{3,0,2,1:T(8,128)(2,1)} %copy.126), calls=%async_computation.1 | async-start | bytes 1835008 | tf_op jit(solution)/shard_map/all_to_all | solution.py:132
  71.0 151.5 %all-reduce.12.cloned.1.call-start = ((), (), s32[]{:S(2)}) async-start(), calls=%async_computation.7 | async-start | bytes 1835008
  83.3 27.8 %copy-start.12 = (bf16[896,2,512]{2,1,0:T(2,128)(2,1)S(1)}, bf16[896,2,512]{2,1,0:T(2,128)(2,1)}, u32[]{:S(2)}) copy-start(bf16[896,2,512]{2,1,0:T(2,128)(2,1)} %param.14) | copy-start | bytes 5505028
  114.7 4.1 copy-start.4
  117.5 4.3 %copy-start.5 = (bf16[2,64,4,128]{3,2,1,0:T(4,128)(2,1)S(1)}, bf16[2,64,4,128]{3,2,1,0:T(4,128)(2,1)}, u32[]{:S(2)}) copy-start(bf16[2,64,4,128]{3,2,1,0:T(4,128)(2,1)} %reshape.100) | copy-start | bytes 393220
  147.4 75.1 %copy-start.10 = (s32[32]{0:T(128)S(1)}, s32[32]{0:T(128)}, u32[]{:S(2)}) copy-start(s32[32]{0:T(128)} %reduce) | copy-start | bytes 388
  149.1 133.9 %all-gather.2.cloned.1.call-start = ((), (), s32[]{:S(2)}) async-start(), calls=%async_computation.5 | async-start | bytes 2064384 | tf_op jit(solution)/shard_map/all_gather | solution.py:189
  223.8 19.9 %copy-start.9 = (s32[8]{0:T(128)S(1)}, s32[8]{0:T(128)}, u32[]{:S(2)}) copy-start(s32[8]{0:T(128)} %copy-done.8) | copy-start | bytes 100
  224.1 20.9 %copy-start.11 = (u32[256]{0:T(256)S(1)}, u32[256]{0:T(256)}, u32[]{:S(2)}) copy-start(u32[256]{0:T(256)} %constant.70) | copy-start | bytes 3076
  244.7 156.5 %all-reduce.10.cloned.1.call-start = ((), (), s32[]{:S(2)}) async-start(), calls=%async_computation.6 | async-start | bytes 3670016
  352.9 56.2 %collective-permute-start.2 = (bf16[32,448]{1,0:T(8,128)(2,1)S(1)}, bf16[32,448]{1,0:T(8,128)(2,1)S(1)}, u32[]{:S(2)}, u32[]{:S(2)}) collective-permute-start(bf16[32,448]{1,0:T(8,128)(2,1)S(1)} %get-tuple-element.19), channel_id=1, source_target_pairs={{0,24},{8,32},{16,40},{24,48},{32,56},{40,64},{48,72},{56,80},{64,... | collective-permute-start | bytes 86024
  354.8 58.1 %collective-permute-start.1 = (bf16[32,448]{1,0:T(8,128)(2,1)S(1)}, bf16[32,448]{1,0:T(8,128)(2,1)S(1)}, u32[]{:S(2)}, u32[]{:S(2)}) collective-permute-start(bf16[32,448]{1,0:T(8,128)(2,1)S(1)} %get-tuple-element.19), channel_id=1, source_target_pairs={{0,16},{8,24},{16,32},{24,40},{32,48},{40,56},{48,64},{56,72},{64,... | collective-permute-start | bytes 86024
  359.9 55.7 %collective-permute-start = (bf16[32,448]{1,0:T(8,128)(2,1)S(1)}, bf16[32,448]{1,0:T(8,128)(2,1)S(1)}, u32[]{:S(2)}, u32[]{:S(2)}) collective-permute-start(bf16[32,448]{1,0:T(8,128)(2,1)S(1)} %get-tuple-element.19), channel_id=1, source_target_pairs={{0,8},{8,16},{16,24},{24,32},{32,40},{40,48},{48,56},{56,64},{64,7... | collective-permute-start | bytes 86024
  365.3 39.3 %collective-permute-start.3 = (bf16[28,448]{1,0:T(8,128)(2,1)S(1)}, bf16[28,448]{1,0:T(8,128)(2,1)S(1)}, u32[]{:S(2)}, u32[]{:S(2)}) collective-permute-start(bf16[28,448]{1,0:T(8,128)(2,1)S(1)} %slice.10), channel_id=1, source_target_pairs={{0,32},{8,40},{16,48},{24,56},{32,64},{40,72},{48,80},{56,88},{64,... | collective-permute-start | bytes 75272
  402.6 18.5 %collective-permute-start.6 = (bf16[32,448]{1,0:T(8,128)(2,1)S(1)}, bf16[32,448]{1,0:T(8,128)(2,1)S(1)}, u32[]{:S(2)}, u32[]{:S(2)}) collective-permute-start(bf16[32,448]{1,0:T(8,128)(2,1)S(1)} %get-tuple-element.20), channel_id=1, source_target_pairs={{0,24},{8,32},{16,40},{24,48},{32,56},{40,64},{48,72},{56,80},{64,... | collective-permute-start | bytes 86024
  404.6 16.5 %collective-permute-start.5 = (bf16[32,448]{1,0:T(8,128)(2,1)S(1)}, bf16[32,448]{1,0:T(8,128)(2,1)S(1)}, u32[]{:S(2)}, u32[]{:S(2)}) collective-permute-start(bf16[32,448]{1,0:T(8,128)(2,1)S(1)} %get-tuple-element.20), channel_id=1, source_target_pairs={{0,16},{8,24},{16,32},{24,40},{32,48},{40,56},{48,64},{56,72},{64,... | collective-permute-start | bytes 86024
  409.1 12.0 %collective-permute-start.4 = (bf16[32,448]{1,0:T(8,128)(2,1)S(1)}, bf16[32,448]{1,0:T(8,128)(2,1)S(1)}, u32[]{:S(2)}, u32[]{:S(2)}) collective-permute-start(bf16[32,448]{1,0:T(8,128)(2,1)S(1)} %get-tuple-element.20), channel_id=1, source_target_pairs={{0,8},{8,16},{16,24},{24,32},{32,40},{40,48},{48,56},{56,64},{64,7... | collective-permute-start | bytes 86024
  412.9 8.2 %collective-permute-start.7 = (bf16[28,448]{1,0:T(8,128)(2,1)S(1)}, bf16[28,448]{1,0:T(8,128)(2,1)S(1)}, u32[]{:S(2)}, u32[]{:S(2)}) collective-permute-start(bf16[28,448]{1,0:T(8,128)(2,1)S(1)} %slice.11), channel_id=1, source_target_pairs={{0,32},{8,40},{16,48},{24,56},{32,64},{40,72},{48,80},{56,88},{64,... | collective-permute-start | bytes 75272
  (6 other events, 6.4 us)
Sparse Core Ops, SparseCore 0:
  15.9 44.0 reduce-scatter.5
  149.2 73.1 all-reduce.11
  244.8 38.1 all-gather.1
  286.5 114.5 all-reduce.9
where the time goes:
time: 430 us; the launch traced here: 429 us
  waiting for transfers between devices  174 us (40%)
  blocking collectives  109 us (25%)
  starting transfers between devices  44.3 us (10%)
  matrix products  42.4 us (10%)
  local copies, waits for them, and re-layouts  35.1 us (8%)
  between operations  16.8 us (4%)
  other arithmetic  8.12 us (2%)
    unnamed x14, waiting for transfers between devices  109 us
    unnamed x1, blocking collectives  62.2 us
    reduce_scatter x1, waiting for transfers between devices, per_device(): lax.psum_scatter(jnp.dot(picked, out_weight, preferred_element_type=jnp.f...  35 us
    unnamed x10, starting transfers between devices  29.1 us
    all_gather x1, blocking collectives, per_device(): piece = lax.all_gather(slices, 'mp', axis=0, tiled=True)  26.8 us
    all_gather x1, waiting for transfers between devices, per_device(): piece = lax.all_gather(slot_grads, 'mp', axis=0, tiled=True)  22.8 us
    all_to_all x1, blocking collectives, per_device(): lax.all_to_all(returned, 'dp', split_axis=1, concat_axis=1, tiled=True)  19.6 us
  transfers between devices with their start and end apart: 14, of which 6 were waited for; matrix products, arithmetic and copies ran while one was open for 22% of the time, Pallas kernels for 0%

commit v1 on v0

v1 whole, which is shorter than its diff:
```python
import functools

import jax
import jax.numpy as jnp
from jax import lax
from jax.experimental import pallas as pl
from jax.experimental.pallas import tpu as pltpu
from jax.sharding import PartitionSpec as P

DH = 128
SPAN = 64
NEIGH = 2
PLACE = 128
CHUNKS = 2
VMEM_LIMIT = 48 * 1024 * 1024

GELU_C = 0.7978845608028654
GELU_A = 0.044715
EPSILON = 1e-06

BF = jnp.bfloat16
F32 = jnp.float32


def dot_nn(a, b):
    return lax.dot_general(a, b, (((1,), (0,)), ((), ())), preferred_element_type=F32)


def dot_nt(a, b):
    return lax.dot_general(a, b, (((1,), (1,)), ((), ())), preferred_element_type=F32)


def dot_tn(a, b):
    return lax.dot_general(a, b, (((0,), (0,)), ((), ())), preferred_element_type=F32)


def call(kernel, outs, *args, scratch=(), flops=0):
    moved = sum(a.size * a.dtype.itemsize for a in args)
    moved += sum(o.size * o.dtype.itemsize for o in outs)
    return pl.pallas_call(
        kernel,
        out_shape=outs,
        scratch_shapes=list(scratch),
        compiler_params=pltpu.CompilerParams(vmem_limit_bytes=VMEM_LIMIT),
        cost_estimate=pl.CostEstimate(flops=flops, bytes_accessed=moved, transcendentals=0),
    )(*args)


def shape_of(shape, dtype=BF):
    return jax.ShapeDtypeStruct(shape, dtype)


def place_kernel(tokens, blocks, got_ref, raw_ref):
    rows, width = got_ref.shape
    wide = width - PLACE
    marks = got_ref[:, wide:]
    spread_rows = lax.broadcasted_iota(jnp.int32, (PLACE, blocks * tokens), 0)
    spread_cols = lax.broadcasted_iota(jnp.int32, (PLACE, blocks * tokens), 1)
    spread = (spread_rows == spread_cols // tokens).astype(BF)
    chosen = dot_nn(marks, spread)
    row_token = lax.broadcasted_iota(jnp.int32, chosen.shape, 0) % tokens
    col_token = lax.broadcasted_iota(jnp.int32, chosen.shape, 1) % tokens
    chosen = jnp.where(row_token == col_token, chosen, 0.0).astype(BF)
    raw_ref[...] = dot_tn(chosen, got_ref[:, :wide]).astype(BF)


def encode_kernel(raw_ref, win_ref, wout_ref, normed_ref, act_ref, slope_ref, part_ref):
    wide = raw_ref[...].astype(F32)
    mean_square = jnp.mean(wide * wide, axis=-1, keepdims=True)
    normed = (wide * lax.rsqrt(mean_square + EPSILON)).astype(BF)
    normed_ref[...] = normed
    pre = dot_nn(normed, win_ref[...])
    square = pre * pre
    tanh_value = jnp.tanh(GELU_C * (pre + GELU_A * square * pre))
    act = (0.5 * pre * (1.0 + tanh_value)).astype(BF)
    act_ref[...] = act
    slope = 0.5 * (1.0 + tanh_value) + 0.5 * pre * (1.0 - tanh_value * tanh_value) * GELU_C * (
        1.0 + 3.0 * GELU_A * square
    )
    slope_ref[...] = slope.astype(BF)
    part_ref[...] = dot_nn(act, wout_ref[...]).astype(BF)


def attend_kernel(spans, enc_ref, kw_ref, vw_ref, q_ref, g_ref, ctx_ref, dq_ref, dk_ref, dv_ref, part_ref):
    scaling = DH ** (-0.5)
    rows = enc_ref.shape[0] // spans
    enc = enc_ref[...]
    keys = dot_nn(enc, kw_ref[...]).astype(BF)
    values = dot_nn(enc, vw_ref[...]).astype(BF)
    heads = keys.shape[1] // DH
    for s in range(spans):
        key_rows = slice(s * rows, (s + 1) * rows)
        q_rows = slice(s * SPAN, (s + 1) * SPAN)
        for h in range(heads):
            cols = slice(h * DH, (h + 1) * DH)
            k = keys[key_rows, cols]
            v = values[key_rows, cols]
            q = q_ref[q_rows, cols]
            g = g_ref[q_rows, cols]
            scores = dot_nt(q, k) * scaling
            peak = jnp.max(scores, axis=-1, keepdims=True)
            weights = jnp.exp(scores - peak)
            probs_wide = weights / jnp.sum(weights, axis=-1, keepdims=True)
            probs = probs_wide.astype(BF)
            ctx_ref[q_rows, cols] = dot_nn(probs, v).astype(BF)
            d_probs = dot_nt(g, v)
            inner = jnp.sum(d_probs * probs_wide, axis=-1, keepdims=True)
            d_scores = (probs_wide * (d_probs - inner) * scaling).astype(BF)
            dq_ref[q_rows, cols] = dot_nn(d_scores, k).astype(BF)
            dk_ref[key_rows, cols] = dot_tn(d_scores, q).astype(BF)
            dv_ref[key_rows, cols] = dot_tn(probs, g).astype(BF)
    part_ref[...] = (dot_nt(dk_ref[...], kw_ref[...]) + dot_nt(dv_ref[...], vw_ref[...])).astype(BF)


def kv_grad_kernel(chunks, *refs):
    encs, dks, dvs = refs[:chunks], refs[chunks : 2 * chunks], refs[2 * chunks : 3 * chunks]
    k_ref, v_ref = refs[3 * chunks :]
    k_ref[...] = sum(dot_tn(e[...], d[...]) for e, d in zip(encs, dks)).astype(BF)
    v_ref[...] = sum(dot_tn(e[...], d[...]) for e, d in zip(encs, dvs)).astype(BF)


def out_grad_kernel(chunks, *refs):
    d_encs, acts = refs[:chunks], refs[chunks : 2 * chunks]
    refs[-1][...] = sum(dot_tn(d[...], a[...]) for d, a in zip(d_encs, acts)).astype(BF)


def in_grad_kernel(chunks, *refs):
    d_encs, normeds, slopes = refs[:chunks], refs[chunks : 2 * chunks], refs[2 * chunks : 3 * chunks]
    wout_ref, total_ref = refs[3 * chunks :]
    total = 0.0
    for d, n, s in zip(d_encs, normeds, slopes):
        d_pre = (dot_nt(d[...], wout_ref[...]) * s[...].astype(F32)).astype(BF)
        total = total + dot_tn(n[...], d_pre)
    total_ref[...] = total.astype(BF)


def gather_mp(piece, ranks):
    rows, width = piece.shape
    copies = jnp.broadcast_to(piece[None], (ranks, rows, width))
    return lax.all_to_all(copies, "mp", 0, 0, tiled=True).reshape(ranks * rows, width)


def scatter_mp(parts, ranks):
    rows, width = parts.shape
    got = lax.all_to_all(parts.reshape(ranks, rows // ranks, width), "mp", 0, 0, tiled=True)
    return jnp.sum(got.astype(F32), axis=0)


def scatter_dp(total, devices):
    rows, width = total.shape
    chips = devices // 2
    core = lax.axis_index("dp") % 2
    split = total.reshape(chips, 2, rows // devices, width)
    give = lax.dynamic_index_in_dim(split, 1 - core, 1, keepdims=False)
    keep = lax.dynamic_index_in_dim(split, core, 1, keepdims=False)
    got = lax.ppermute(give, "dp", [(i, i ^ 1) for i in range(devices)])
    pair = (keep.astype(F32) + got.astype(F32)).astype(BF)
    groups = [[chip * 2 + c for chip in range(chips)] for c in range(2)]
    every = lax.all_to_all(pair, "dp", 0, 0, axis_index_groups=groups, tiled=True)
    return jnp.sum(every.astype(F32), axis=0)


def per_device(queries, neighbours, targets, counts, in_weight, out_weight, kv_weight, d_context):
    length, holding, width = neighbours.shape
    owners = lax.axis_size("dp")
    ranks = lax.axis_size("mp")
    tokens = length // ranks
    token_rows, columns = queries.shape
    hidden = in_weight.shape[1]
    spans = token_rows // SPAN
    blocks = NEIGH * spans
    my_rank = lax.axis_index("mp")

    own = lax.dynamic_slice_in_dim(neighbours, my_rank * tokens, tokens, 0).reshape(tokens * holding, width)
    is_live = jnp.arange(holding, dtype=jnp.int32) < counts[0]
    dest = jnp.where(is_live, targets // blocks, -1)
    place = targets % blocks
    marks = jnp.arange(PLACE, dtype=jnp.int32)[None, :] == jnp.tile(place, tokens)[:, None]
    payload = jnp.concatenate([own, marks.astype(BF)], axis=1)
    row_ids = jnp.arange(owners * tokens, dtype=jnp.int32)
    col_ids = jnp.arange(tokens * holding, dtype=jnp.int32)
    pick = jnp.logical_and(
        (row_ids // tokens)[:, None] == jnp.tile(dest, tokens)[None, :],
        (row_ids % tokens)[:, None] == (col_ids // holding)[None, :],
    ).astype(BF)
    sent = dot_nn(pick, payload).astype(BF).reshape(owners, tokens, width + PLACE)
    got = lax.all_to_all(sent, "dp", 0, 0, tiled=True).reshape(owners * tokens, width + PLACE)
    (raw,) = call(
        functools.partial(place_kernel, tokens, blocks),
        [shape_of((blocks * tokens, width))],
        got,
        flops=2 * owners * tokens * blocks * tokens * width,
    )

    kw = kv_weight[:, 0, :]
    vw = kv_weight[:, 1, :]

    per_chunk = spans // CHUNKS
    piece_rows = blocks * tokens // CHUNKS
    chunk_rows = piece_rows * ranks
    raws = [raw[c * piece_rows : (c + 1) * piece_rows] for c in range(CHUNKS)]
    kept = []
    parts = []
    for c in range(CHUNKS):
        every = gather_mp(raws[c], ranks)
        if per_chunk > 1:
            every = (
                every.reshape(ranks, per_chunk, -1, width).transpose(1, 0, 2, 3).reshape(chunk_rows, width)
            )
        normed, act, slope, part = call(
            encode_kernel,
            [
                shape_of((chunk_rows, width)),
                shape_of((chunk_rows, hidden)),
                shape_of((chunk_rows, hidden)),
                shape_of((chunk_rows, width)),
            ],
            every,
            in_weight,
            out_weight,
            flops=4 * chunk_rows * width * hidden,
        )
        kept.append((normed, act, slope))
        parts.append(part)
    pieces = []
    for c in range(CHUNKS):
        part = parts[c]
        summed = scatter_mp(part, ranks)
        pieces.append((raws[c].astype(F32) + summed).astype(BF))
    encs = [gather_mp(p, ranks) for p in pieces]
    results = []
    for c in range(CHUNKS):
        q_rows = slice(c * per_chunk * SPAN, (c + 1) * per_chunk * SPAN)
        results.append(
            call(
                functools.partial(attend_kernel, per_chunk),
                [
                    shape_of((per_chunk * SPAN, columns)),
                    shape_of((per_chunk * SPAN, columns)),
                    shape_of((chunk_rows, columns)),
                    shape_of((chunk_rows, columns)),
                    shape_of((chunk_rows, width)),
                ],
                encs[c],
                kw,
                vw,
                queries[q_rows],
                d_context[q_rows],
                flops=8 * chunk_rows * width * columns,
            )
        )
    d_encs = [gather_mp(scatter_mp(r[4], ranks).astype(BF), ranks) for r in results]
    kv_k, kv_v = call(
        functools.partial(kv_grad_kernel, CHUNKS),
        [shape_of((width, columns))] * 2,
        *encs,
        *[r[2] for r in results],
        *[r[3] for r in results],
        flops=4 * CHUNKS * chunk_rows * width * columns,
    )
    grad_kv = scatter_dp(jnp.concatenate([kv_k, kv_v], axis=1), owners)
    (out_total,) = call(
        functools.partial(out_grad_kernel, CHUNKS),
        [shape_of((width, hidden))],
        *d_encs,
        *[k[1] for k in kept],
        flops=2 * CHUNKS * chunk_rows * width * hidden,
    )
    grad_out_t = scatter_dp(out_total, owners)
    (in_total,) = call(
        functools.partial(in_grad_kernel, CHUNKS),
        [shape_of((width, hidden))],
        *d_encs,
        *[k[0] for k in kept],
        *[k[2] for k in kept],
        out_weight,
        flops=4 * CHUNKS * chunk_rows * width * hidden,
    )
    grad_in = scatter_dp(in_total, owners)
    context = jnp.concatenate([r[0] for r in results], axis=0)
    d_queries = jnp.concatenate([r[1] for r in results], axis=0)
    return (
        context,
        d_queries,
        grad_kv.reshape(width // owners, 2, columns),
        grad_in,
        grad_out_t.T,
    )


def solution(mesh):
    placed = (
        P("dp", "mp"),
        P(None, "dp", None),
        P("dp"),
        P("dp"),
        P(None, "mp"),
        P("mp", None),
        P(None, None, "mp"),
        P("dp", "mp"),
    )
    return jax.shard_map(
        per_device,
        mesh=mesh,
        in_specs=placed,
        out_specs=(P("dp", "mp"), P("dp", "mp"), P("dp", None, "mp"), P("dp", "mp"), P("mp", "dp")),
        check_vma=False,
    )
```

time: 430 us -> 300 us (0.70)
  waiting for transfers between devices: 174 us -> 79.5 us
  blocking collectives: 109 us -> 66.2 us
  matrix products: 42.4 us -> 0.49 us
  local copies, waits for them, and re-layouts: 35.1 us -> 57.1 us
  Pallas kernels: 0 us -> 15.3 us
  between operations: 16.8 us -> 1.9 us
  starting transfers between devices: 44.3 us -> 56.8 us
  other arithmetic: 8.12 us -> 18.4 us
    unnamed x14 -> x0, waiting for transfers between devices: 109 us -> none
    all_to_all x2 -> x11, waiting for transfers between devices: 7.24 us -> 79.5 us  [the longest x4 46 us: scatter_mp(): lax.all_to_all(parts.reshape(ranks, rows // ranks, width), 'mp', 0, 0, ti...]
    unnamed x1 -> x0, blocking collectives: 62.2 us -> none
    all_to_all x1 -> x3, blocking collectives: 19.6 us -> 66.2 us  [the longest x2 45.2 us: gather_mp(): lax.all_to_all(copies, 'mp', 0, 0, tiled=True).reshape(ranks * rows, width)]
    dot_general x17 -> x1, matrix products: 42.4 us -> 0.49 us  [dot_nn(): lax.dot_general(a, b, (((1,), (0,)), ((), ())), preferred_element_type=F32)]
    all_to_all x2 -> x11, starting transfers between devices: 15.1 us -> 56.2 us  [the longest x3 21.2 us: scatter_dp(): lax.all_to_all(pair, 'dp', 0, 0, axis_index_groups=groups, tiled=True)]
    reduce_scatter x1 -> x0, waiting for transfers between devices: 35 us -> none  [per_device(): lax.psum_scatter(jnp.dot(picked, out_weight, preferred_element_type=jnp.f...]
    unnamed x10 -> x0, starting transfers between devices: 29.1 us -> none
  transfers between devices with their start and end apart: 14 -> 14, of which waited for: 6 -> 9; matrix products, arithmetic and copies ran while one was open for 22% -> 14% of each run, Pallas kernels for 0% -> 5%
where the time goes in v1:
time: 300 us; the launch traced here: 296 us
  waiting for transfers between devices  79.5 us (26%)
  blocking collectives  66.2 us (22%)
  local copies, waits for them, and re-layouts  57.1 us (19%)
  starting transfers between devices  56.8 us (19%)
  other arithmetic  18.4 us (6%)
  Pallas kernels  15.3 us (5%)
    all_to_all x4, waiting for transfers between devices, scatter_mp(): lax.all_to_all(parts.reshape(ranks, rows // ranks, width), 'mp', 0, 0, ti...  46 us
    all_to_all x2, blocking collectives, gather_mp(): lax.all_to_all(copies, 'mp', 0, 0, tiled=True).reshape(ranks * rows, width)  45.2 us
    unnamed x99, local copies, waits for them, and re-layouts  31.7 us
    all_to_all x4, waiting for transfers between devices, gather_mp(): lax.all_to_all(copies, 'mp', 0, 0, tiled=True).reshape(ranks * rows, width)  25.5 us
    all_to_all x3, starting transfers between devices, scatter_dp(): lax.all_to_all(pair, 'dp', 0, 0, axis_index_groups=groups, tiled=True)  21.2 us
    all_to_all x1, blocking collectives, per_device(): lax.all_to_all(sent, 'dp', 0, 0, tiled=True)  21.1 us
    all_to_all x4, starting transfers between devices, gather_mp(): lax.all_to_all(copies, 'mp', 0, 0, tiled=True).reshape(ranks * rows, width)  18.8 us
    all_to_all x4, starting transfers between devices, scatter_mp(): lax.all_to_all(parts.reshape(ranks, rows // ranks, width), 'mp', 0, 0, ti...  16.3 us
  transfers between devices with their start and end apart: 14, of which 9 were waited for; matrix products, arithmetic and copies ran while one was open for 14% of the time, Pallas kernels for 5%

profile of v1, /device:TPU:12, one launch (start us, length us, event | category | flops | bytes accessed | tf_op | source)
XLA Modules:
  0.0 295.7 jit_solution(1341192278829559293)
XLA Ops:
  2.9 21.1 %all_to_all.70 = bf16[32,16,1024]{2,1,0:T(8,128)(2,1)S(1)} all-to-all(bf16[32,16,1024]{2,1,0:T(8,128)(2,1)S(1)} %bitcast.49), channel_id=1, replica_groups=mesh['dp'=32,'mp'=8] {'dp'}, dimensions={0} | all-to-all | bytes 2097152 | tf_op jit(solution)/shard_map/all_to_all | solution.py:187
  25.2 25.5 %all_to_all.71 = bf16[8,32,896]{2,1,0:T(8,128)(2,1)} all-to-all(bf16[8,32,896]{2,1,0:T(8,128)(2,1)S(1)} %broadcast_in_dim.16), channel_id=1, replica_groups=mesh['dp'=32,'mp'=8] {'mp'}, dimensions={0} | all-to-all | bytes 917504 | tf_op jit(solution)/shard_map/all_to_all | solution.py:140
  51.6 4.1 %all-to-all-start.1 = ((bf16[8,32,896]{2,1,0:T(8,128)(2,1)}), bf16[8,32,896]{2,1,0:T(8,128)(2,1)}, u32[]{:S(2)}, u32[]{:S(2)}) async-start(bf16[8,32,896]{2,1,0:T(8,128)(2,1)} %broadcast_in_dim.14), calls=%async_computation.1 | async-start | bytes 917504 | tf_op jit(solution)/shard_map/all_to_all | solution.py:140
  62.3 10.0 %all-to-all-done.1 = bf16[8,32,896]{2,1,0:T(8,128)(2,1)} async-done(((bf16[8,32,896]{2,1,0:T(8,128)(2,1)}), bf16[8,32,896]{2,1,0:T(8,128)(2,1)}, u32[]{:S(2)}, u32[]{:S(2)}) %all-to-all-start.1) | async-done | bytes 458784 | tf_op jit(solution)/shard_map/all_to_all | solution.py:140
  72.3 4.1 %all-to-all-start.5 = ((bf16[8,32,896]{2,1,0:T(8,128)(2,1)}), bf16[8,32,896]{2,1,0:T(8,128)(2,1)}, u32[]{:S(2)}, u32[]{:S(2)}) async-start(bf16[8,32,896]{2,1,0:T(8,128)(2,1)} %bitcast.46), calls=%async_computation.5 | async-start | bytes 917504 | tf_op jit(solution)/shard_map/all_to_all | solution.py:145
  81.5 11.4 %all-to-all-done.5 = bf16[8,32,896]{2,1,0:T(8,128)(2,1)} async-done(((bf16[8,32,896]{2,1,0:T(8,128)(2,1)}), bf16[8,32,896]{2,1,0:T(8,128)(2,1)}, u32[]{:S(2)}, u32[]{:S(2)}) %all-to-all-start.5) | async-done | bytes 458784 | tf_op jit(solution)/shard_map/all_to_all | solution.py:145
  93.0 3.5 %all-to-all-start.2 = ((bf16[8,32,896]{2,1,0:T(8,128)(2,1)}), bf16[8,32,896]{2,1,0:T(8,128)(2,1)S(1)}, u32[]{:S(2)}, u32[]{:S(2)}) async-start(bf16[8,32,896]{2,1,0:T(8,128)(2,1)} %bitcast.48), calls=%async_computation.2 | async-start | bytes 917504 | tf_op jit(solution)/shard_map/all_to_all | solution.py:145
  97.5 15.4 %all-to-all-done.2 = bf16[8,32,896]{2,1,0:T(8,128)(2,1)S(1)} async-done(((bf16[8,32,896]{2,1,0:T(8,128)(2,1)}), bf16[8,32,896]{2,1,0:T(8,128)(2,1)S(1)}, u32[]{:S(2)}, u32[]{:S(2)}) %all-to-all-start.2) | async-done | bytes 458784 | tf_op jit(solution)/shard_map/all_to_all | solution.py:145
  113.1 19.6 %all_to_all.72 = bf16[8,32,896]{2,1,0:T(8,128)(2,1)} all-to-all(bf16[8,32,896]{2,1,0:T(8,128)(2,1)S(1)} %broadcast_in_dim.15), channel_id=1, replica_groups=mesh['dp'=32,'mp'=8] {'mp'}, dimensions={0} | all-to-all | bytes 917504 | tf_op jit(solution)/shard_map/all_to_all | solution.py:140
  133.5 4.1 %all-to-all-start.6 = ((bf16[8,32,896]{2,1,0:T(8,128)(2,1)}), bf16[8,32,896]{2,1,0:T(8,128)(2,1)}, u32[]{:S(2)}, u32[]{:S(2)}) async-start(bf16[8,32,896]{2,1,0:T(8,128)(2,1)} %broadcast_in_dim.17), calls=%async_computation.6 | async-start | bytes 917504 | tf_op jit(solution)/shard_map/all_to_all | solution.py:140
  137.7 5.2 %fusion.22 = (bf16[896,1,512]{2,1,0:T(2,128)(2,1)S(1)}, bf16[896,1,512]{2,1,0:T(2,128)(2,1)S(1)}) fusion(bf16[896,2,512]{2,1,0:T(2,128)(2,1)} %param.14), kind=kLoop, calls=%fused_computation.58 | loop fusion | bytes 3670016 | tf_op jit(solution)/shard_map/slice | solution.py:196
  154.1 5.2 %all-to-all-start.8 = ((bf16[8,32,896]{2,1,0:T(8,128)(2,1)}), bf16[8,32,896]{2,1,0:T(8,128)(2,1)}, u32[]{:S(2)}, u32[]{:S(2)}) async-start(bf16[8,32,896]{2,1,0:T(8,128)(2,1)} %bitcast.45), calls=%async_computation.8 | async-start | bytes 917504 | tf_op jit(solution)/shard_map/all_to_all | solution.py:145
  162.1 4.2 %shard_map.123 = (bf16[64,512]{1,0:T(8,128)(2,1)S(1)}, bf16[64,512]{1,0:T(8,128)(2,1)S(1)}, bf16[256,512]{1,0:T(8,128)(2,1)S(1)}, bf16[256,512]{1,0:T(8,128)(2,1)S(1)}, bf16[256,896]{1,0:T(8,128)(2,1)S(1)}) custom-call(bf16[256,896]{1,0:T(8,128)(2,1)} %bitcast.11.enc_ref.refs_1_, bf16[896,512]{1,0:T(8,128)(2,1)S(1)} %copy-done.8, ...), custom_call_target="tpu_custom_call" | custom-call | flops 939524096 | bytes 3538944 | tf_op jit(solution)/shard_map/pallas_call | solution.py:40
  169.7 5.5 %all-to-all-done.8 = bf16[8,32,896]{2,1,0:T(8,128)(2,1)} async-done(((bf16[8,32,896]{2,1,0:T(8,128)(2,1)}), bf16[8,32,896]{2,1,0:T(8,128)(2,1)}, u32[]{:S(2)}, u32[]{:S(2)}) %all-to-all-start.8) | async-done | bytes 458784 | tf_op jit(solution)/shard_map/all_to_all | solution.py:145
  175.3 3.5 %all-to-all-start.10 = ((bf16[8,32,896]{2,1,0:T(8,128)(2,1)}), bf16[8,32,896]{2,1,0:T(8,128)(2,1)S(1)}, u32[]{:S(2)}, u32[]{:S(2)}) async-start(bf16[8,32,896]{2,1,0:T(8,128)(2,1)} %bitcast.47), calls=%async_computation.10 | async-start | bytes 917504 | tf_op jit(solution)/shard_map/all_to_all | solution.py:145
  180.5 13.6 %all-to-all-done.10 = bf16[8,32,896]{2,1,0:T(8,128)(2,1)S(1)} async-done(((bf16[8,32,896]{2,1,0:T(8,128)(2,1)}), bf16[8,32,896]{2,1,0:T(8,128)(2,1)S(1)}, u32[]{:S(2)}, u32[]{:S(2)}) %all-to-all-start.10) | async-done | bytes 458784 | tf_op jit(solution)/shard_map/all_to_all | solution.py:145
  195.7 3.5 %all-to-all-start.9 = ((bf16[8,32,896]{2,1,0:T(8,128)(2,1)}), bf16[8,32,896]{2,1,0:T(8,128)(2,1)S(1)}, u32[]{:S(2)}, u32[]{:S(2)}) async-start(bf16[8,32,896]{2,1,0:T(8,128)(2,1)} %broadcast_in_dim.18), calls=%async_computation.9 | async-start | bytes 917504 | tf_op jit(solution)/shard_map/all_to_all | solution.py:140
  206.7 3.7 %reshape.121 = bf16[16,2,28,1024]{3,2,1,0:T(8,128)(2,1)} reshape(bf16[896,1024]{1,0:T(8,128)(2,1)} %pad_maximum_fusion) | data formatting | bytes 3670016 | tf_op jit(solution)/shard_map/reshape | solution.py:153
  215.5 7.1 %all-to-all-start.11 = ((bf16[8,32,896]{2,1,0:T(8,128)(2,1)}), bf16[8,32,896]{2,1,0:T(8,128)(2,1)S(1)}, u32[]{:S(2)}, u32[]{:S(2)}) async-start(bf16[8,32,896]{2,1,0:T(8,128)(2,1)} %broadcast_in_dim.19), calls=%async_computation.11 | async-start | bytes 917504 | tf_op jit(solution)/shard_map/all_to_all | solution.py:140
  225.8 13.7 %all-to-all-done.11 = bf16[8,32,896]{2,1,0:T(8,128)(2,1)S(1)} async-done(((bf16[8,32,896]{2,1,0:T(8,128)(2,1)}), bf16[8,32,896]{2,1,0:T(8,128)(2,1)S(1)}, u32[]{:S(2)}, u32[]{:S(2)}) %all-to-all-start.11) | async-done | bytes 458784 | tf_op jit(solution)/shard_map/all_to_all | solution.py:140
  239.4 6.9 %all-to-all-start.7 = ((bf16[16,28,1024]{2,1,0:T(8,128)(2,1)}), bf16[16,28,1024]{2,1,0:T(8,128)(2,1)}, u32[]{:S(2)}, u32[]{:S(2)}) async-start(bf16[16,28,1024]{2,1,0:T(8,128)(2,1)} %fusion), calls=%async_computation.7 | async-start | bytes 2097152 | tf_op jit(solution)/shard_map/all_to_all | solution.py:159
  265.3 7.4 %all-to-all-start.13 = ((bf16[16,28,448]{2,1,0:T(8,128)(2,1)}), bf16[16,28,448]{2,1,0:T(8,128)(2,1)}, u32[]{:S(2)}, u32[]{:S(2)}) async-start(bf16[16,28,448]{2,1,0:T(8,128)(2,1)} %fusion.1), calls=%async_computation.13 | async-start | bytes 1048576 | tf_op jit(solution)/shard_map/all_to_all | solution.py:159
  275.3 5.7 %all-to-all-done.13 = bf16[16,28,448]{2,1,0:T(8,128)(2,1)} async-done(((bf16[16,28,448]{2,1,0:T(8,128)(2,1)}), bf16[16,28,448]{2,1,0:T(8,128)(2,1)}, u32[]{:S(2)}, u32[]{:S(2)}) %all-to-all-start.13) | async-done | bytes 401440 | tf_op jit(solution)/shard_map/all_to_all | solution.py:159
  281.0 6.9 %all-to-all-start.12 = ((bf16[16,28,448]{2,1,0:T(8,128)(2,1)}), bf16[16,28,448]{2,1,0:T(8,128)(2,1)S(1)}, u32[]{:S(2)}, u32[]{:S(2)}) async-start(bf16[16,28,448]{2,1,0:T(8,128)(2,1)} %fusion.2), calls=%async_computation.12 | async-start | bytes 1048576 | tf_op jit(solution)/shard_map/all_to_all | solution.py:159
  (156 shorter events, 82.9 us)
Async XLA Ops:
  25.2 32.0 %copy-start.1 = (bf16[448,896]{1,0:T(8,128)(2,1)S(1)}, bf16[448,896]{1,0:T(8,128)(2,1)}, u32[]{:S(2)}) copy-start(bf16[448,896]{1,0:T(8,128)(2,1)} %refs_6_.1) | copy-start | bytes 2408452
  51.6 20.7 %all-to-all-start.1 = ((bf16[8,32,896]{2,1,0:T(8,128)(2,1)}), bf16[8,32,896]{2,1,0:T(8,128)(2,1)}, u32[]{:S(2)}, u32[]{:S(2)}) async-start(bf16[8,32,896]{2,1,0:T(8,128)(2,1)} %broadcast_in_dim.14), calls=%async_computation.1 | async-start | bytes 917504 | tf_op jit(solution)/shard_map/all_to_all | solution.py:140
  72.3 20.7 %all-to-all-start.5 = ((bf16[8,32,896]{2,1,0:T(8,128)(2,1)}), bf16[8,32,896]{2,1,0:T(8,128)(2,1)}, u32[]{:S(2)}, u32[]{:S(2)}) async-start(bf16[8,32,896]{2,1,0:T(8,128)(2,1)} %bitcast.46), calls=%async_computation.5 | async-start | bytes 917504 | tf_op jit(solution)/shard_map/all_to_all | solution.py:145
  81.5 31.5 %copy-start.6 = (bf16[64,896]{1,0:T(8,128)(2,1)S(1)}, bf16[64,896]{1,0:T(8,128)(2,1)}, u32[]{:S(2)}) copy-start(bf16[64,896]{1,0:T(8,128)(2,1)} %copy-done.5) | copy-start | bytes 344068
  93.0 19.9 %all-to-all-start.2 = ((bf16[8,32,896]{2,1,0:T(8,128)(2,1)}), bf16[8,32,896]{2,1,0:T(8,128)(2,1)S(1)}, u32[]{:S(2)}, u32[]{:S(2)}) async-start(bf16[8,32,896]{2,1,0:T(8,128)(2,1)} %bitcast.48), calls=%async_computation.2 | async-start | bytes 917504 | tf_op jit(solution)/shard_map/all_to_all | solution.py:145
  133.5 20.6 %all-to-all-start.6 = ((bf16[8,32,896]{2,1,0:T(8,128)(2,1)}), bf16[8,32,896]{2,1,0:T(8,128)(2,1)}, u32[]{:S(2)}, u32[]{:S(2)}) async-start(bf16[8,32,896]{2,1,0:T(8,128)(2,1)} %broadcast_in_dim.17), calls=%async_computation.6 | async-start | bytes 917504 | tf_op jit(solution)/shard_map/all_to_all | solution.py:140
  137.6 5.3 %copy-start.47 = (bf16[128,512]{1,0:T(8,128)(2,1)S(1)}, bf16[128,512]{1,0:T(8,128)(2,1)}, u32[]{:S(2)}) copy-start(bf16[128,512]{1,0:T(8,128)(2,1)} %param.15) | copy-start | bytes 393220
  137.6 5.3 %copy-start.48 = (bf16[128,512]{1,0:T(8,128)(2,1)S(1)}, bf16[128,512]{1,0:T(8,128)(2,1)}, u32[]{:S(2)}) copy-start(bf16[128,512]{1,0:T(8,128)(2,1)} %param.8) | copy-start | bytes 393220
  154.1 21.2 %all-to-all-start.8 = ((bf16[8,32,896]{2,1,0:T(8,128)(2,1)}), bf16[8,32,896]{2,1,0:T(8,128)(2,1)}, u32[]{:S(2)}, u32[]{:S(2)}) async-start(bf16[8,32,896]{2,1,0:T(8,128)(2,1)} %bitcast.45), calls=%async_computation.8 | async-start | bytes 917504 | tf_op jit(solution)/shard_map/all_to_all | solution.py:145
  169.7 29.5 %copy-start.10 = (bf16[8,32,896]{2,1,0:T(8,128)(2,1)S(1)}, bf16[8,32,896]{2,1,0:T(8,128)(2,1)}, u32[]{:S(2)}) copy-start(bf16[8,32,896]{2,1,0:T(8,128)(2,1)} %all_to_all.72) | copy-start | bytes 1376260
  175.3 18.8 %all-to-all-start.10 = ((bf16[8,32,896]{2,1,0:T(8,128)(2,1)}), bf16[8,32,896]{2,1,0:T(8,128)(2,1)S(1)}, u32[]{:S(2)}, u32[]{:S(2)}) async-start(bf16[8,32,896]{2,1,0:T(8,128)(2,1)} %bitcast.47), calls=%async_computation.10 | async-start | bytes 917504 | tf_op jit(solution)/shard_map/all_to_all | solution.py:145
  195.7 18.2 %all-to-all-start.9 = ((bf16[8,32,896]{2,1,0:T(8,128)(2,1)}), bf16[8,32,896]{2,1,0:T(8,128)(2,1)S(1)}, u32[]{:S(2)}, u32[]{:S(2)}) async-start(bf16[8,32,896]{2,1,0:T(8,128)(2,1)} %broadcast_in_dim.18), calls=%async_computation.9 | async-start | bytes 917504 | tf_op jit(solution)/shard_map/all_to_all | solution.py:140
  210.4 2.8 copy-start.46
  213.2 9.4 %collective-permute-start = (bf16[16,28,1024]{2,0,1:T(8,128)(2,1)}, bf16[16,28,1024]{2,0,1:T(8,128)(2,1)}, u32[]{:S(2)}, u32[]{:S(2)}) collective-permute-start(bf16[16,28,1024]{2,0,1:T(8,128)(2,1)} %bitcast.35), channel_id=1, source_target_pairs={{0,8},{8,0},{16,24},{24,16},{32,40},{40,32},{48,56},{56,48},{64,72... | collective-permute-start | bytes 2752520 | tf_op jit(solution)/shard_map/ppermute | solution.py:156
  215.5 23.9 %all-to-all-start.11 = ((bf16[8,32,896]{2,1,0:T(8,128)(2,1)}), bf16[8,32,896]{2,1,0:T(8,128)(2,1)S(1)}, u32[]{:S(2)}, u32[]{:S(2)}) async-start(bf16[8,32,896]{2,1,0:T(8,128)(2,1)} %broadcast_in_dim.19), calls=%async_computation.11 | async-start | bytes 917504 | tf_op jit(solution)/shard_map/all_to_all | solution.py:140
  239.4 25.8 %all-to-all-start.7 = ((bf16[16,28,1024]{2,1,0:T(8,128)(2,1)}), bf16[16,28,1024]{2,1,0:T(8,128)(2,1)}, u32[]{:S(2)}, u32[]{:S(2)}) async-start(bf16[16,28,1024]{2,1,0:T(8,128)(2,1)} %fusion), calls=%async_computation.7 | async-start | bytes 2097152 | tf_op jit(solution)/shard_map/all_to_all | solution.py:159
  254.0 9.1 %collective-permute-start.2 = (bf16[16,28,448]{2,1,0:T(8,128)(2,1)}, bf16[16,28,448]{2,1,0:T(8,128)(2,1)}, u32[]{:S(2)}, u32[]{:S(2)}) collective-permute-start(bf16[16,28,448]{2,1,0:T(8,128)(2,1)} %dynamic-slice_bitcast_fusion), channel_id=1, source_target_pairs={{0,8},{8,0},{16,24},{24,16},{32,40},{40,32},{48,56},{56,48},{64,72... | collective-permute-start | bytes 1204232 | tf_op jit(solution)/shard_map/ppermute | solution.py:156
  261.7 10.9 %copy-start.32 = (bf16[64,512]{1,0:T(8,128)(2,1)S(1)}, bf16[64,512]{1,0:T(8,128)(2,1)}, u32[]{:S(2)}) copy-start(bf16[64,512]{1,0:T(8,128)(2,1)} %copy-done.31) | copy-start | bytes 196612
  261.7 10.9 %copy-start.34 = (bf16[64,512]{1,0:T(8,128)(2,1)S(1)}, bf16[64,512]{1,0:T(8,128)(2,1)}, u32[]{:S(2)}) copy-start(bf16[64,512]{1,0:T(8,128)(2,1)} %copy-done.33) | copy-start | bytes 196612
  262.6 10.7 %collective-permute-start.1 = (bf16[16,28,448]{2,1,0:T(8,128)(2,1)}, bf16[16,28,448]{2,1,0:T(8,128)(2,1)}, u32[]{:S(2)}, u32[]{:S(2)}) collective-permute-start(bf16[16,28,448]{2,1,0:T(8,128)(2,1)} %dynamic-slice_bitcast_fusion.1), channel_id=1, source_target_pairs={{0,8},{8,0},{16,24},{24,16},{32,40},{40,32},{48,56},{56,48},{64,72... | collective-permute-start | bytes 1204232 | tf_op jit(solution)/shard_map/ppermute | solution.py:156
  265.3 22.7 %copy-start.28 = (bf16[64,512]{1,0:T(8,128)(2,1)S(1)}, bf16[64,512]{1,0:T(8,128)(2,1)}, u32[]{:S(2)}) copy-start(bf16[64,512]{1,0:T(8,128)(2,1)} %copy-done.27) | copy-start | bytes 196612
  265.3 22.7 %copy-start.30 = (bf16[64,512]{1,0:T(8,128)(2,1)S(1)}, bf16[64,512]{1,0:T(8,128)(2,1)}, u32[]{:S(2)}) copy-start(bf16[64,512]{1,0:T(8,128)(2,1)} %copy-done.29) | copy-start | bytes 196612
  265.3 15.7 %all-to-all-start.13 = ((bf16[16,28,448]{2,1,0:T(8,128)(2,1)}), bf16[16,28,448]{2,1,0:T(8,128)(2,1)}, u32[]{:S(2)}, u32[]{:S(2)}) async-start(bf16[16,28,448]{2,1,0:T(8,128)(2,1)} %fusion.1), calls=%async_computation.13 | async-start | bytes 1048576 | tf_op jit(solution)/shard_map/all_to_all | solution.py:159
  281.0 14.0 %all-to-all-start.12 = ((bf16[16,28,448]{2,1,0:T(8,128)(2,1)}), bf16[16,28,448]{2,1,0:T(8,128)(2,1)S(1)}, u32[]{:S(2)}, u32[]{:S(2)}) async-start(bf16[16,28,448]{2,1,0:T(8,128)(2,1)} %fusion.2), calls=%async_computation.12 | async-start | bytes 1048576 | tf_op jit(solution)/shard_map/all_to_all | solution.py:159
  (39 other events, 34.2 us)
